TPU v7x, 32 devices: a whole 2x2x4 slice. The times are simulated.
32 devices in a mesh: dp: 2 (over y), ctx: 16 (over z, x, core).
Axes of the slice: x: 2, y: 2, z: 4, core: 2. Of those that a mesh axis runs over, the one named last changes fastest.
Arguments:
- queries: bfloat16 [2, 2048, 1024], P('dp', 'ctx'), may hold values from -6 to 6
- keys: bfloat16 [2, 2048, 1024], P('dp', 'ctx'), may hold values from -0.5390625 to 0.5390625
- values: bfloat16 [2, 2048, 1024], P('dp', 'ctx'), may hold values from -6 to 6
- gain: float32 [1024], replicated, may hold values from 0.1 to 1.9
- grad_out: bfloat16 [2, 2048, 1024], P('dp', 'ctx'), may hold values from -16 to 16
Outputs:
- output: bfloat16 [2, 2048, 1024], P('dp', 'ctx')
- grad_queries: bfloat16 [2, 2048, 1024], P('dp', 'ctx')
- grad_keys: bfloat16 [2, 2048, 1024], P('dp', 'ctx')
- grad_values: bfloat16 [2, 2048, 1024], P('dp', 'ctx')
- grad_gain: float32 [1024], replicated
All inputs are finite; a program needn't handle non-finite values.
Results may differ from a plain program's by a relative error of at most 0.006.
Values sent between devices are 32-bit elements; how exact they have to be, the bound alone decides.
A program may use at most 128 MiB of HBM per device.

v0:
```python
import functools

import jax
import jax.numpy as jnp
from jax import lax
from jax.experimental import pallas as pl
from jax.experimental.pallas import tpu as pltpu
from jax.sharding import PartitionSpec as P

HEAD_DIM = 64
GROUP = 128
LANES = 2 * HEAD_DIM
F32 = jnp.float32
BF16 = jnp.bfloat16
MESH = pl.DeviceIdType.MESH


def nn(a, b):
    return lax.dot_general(a, b, (((1,), (0,)), ((), ())), preferred_element_type=F32)


def nt(a, b):
    return lax.dot_general(a, b, (((1,), (1,)), ((), ())), preferred_element_type=F32)


def tn(a, b):
    return lax.dot_general(a, b, (((0,), (0,)), ((), ())), preferred_element_type=F32)


def first_head(rows):
    return lax.broadcasted_iota(jnp.int32, (rows, LANES), 1) < HEAD_DIM


def by_head(x):
    mask = first_head(x.shape[0])
    zero = jnp.zeros_like(x)
    return jnp.concatenate([jnp.where(mask, x, zero), jnp.where(mask, zero, x)], 0)


def pack(square):
    mask = first_head(HEAD_DIM)
    return jnp.where(mask, square[:HEAD_DIM], square[HEAD_DIM:])


def unpack(packed):
    mask = first_head(HEAD_DIM)
    zero = jnp.zeros_like(packed)
    both = [jnp.where(mask, packed, zero), jnp.where(mask, zero, packed)]
    return jnp.concatenate(both, 0).astype(BF16)


def side_by_side(stacked):
    return jnp.concatenate([stacked[:GROUP], stacked[GROUP:]], 1)


def flips(count):
    return sorted(range(1, count), key=lambda mask: (-(mask // 2).bit_count(), mask % 2, mask))


def flipped(place, mask, count):
    out = 0
    bit = 1
    while bit < count:
        out = out + lax.rem(place // bit + (1 if mask & bit else 0), 2) * bit
        bit *= 2
    return out


def scan_kernel(
    n, ndp, q_hbm, k_hbm, v_hbm, gain_hbm, g_hbm,
    k, v, o_out, gq_out, gk_part, gv_part, later,
    q, g, gain_ref, attn, grad_attn, scores, q_turned,
    kv, kv_in, prefix, state, qd, qd_in, suffix, sums, carry, gains,
    in_sems, send_sems, recv_sems, carry_send, carry_recv, gain_send, gain_recv,
):
    me = lax.axis_index("ctx")
    row = lax.axis_index("dp")
    width = q.shape[1]
    pairs = width // LANES
    chunks = kv.shape[0]
    group = pairs // chunks
    share = kv.shape[2]
    slots = HEAD_DIM // share
    half = n // 2
    upper = me // half
    place = lax.rem(me, half)
    other = lax.rem(me + half, n)

    barrier = pltpu.get_barrier_semaphore()
    loads = []
    arrays = (k_hbm.at[0], k), (v_hbm.at[0], v), (q_hbm.at[0], q), (g_hbm.at[0], g)
    for i, (src, dst) in enumerate(arrays + ((gain_hbm, gain_ref),)):
        loads.append(pltpu.make_async_copy(src, dst, in_sems.at[i]))
        loads[-1].start()

    mates = [flipped(place, mask, half) for mask in flips(half)]
    twins = [(lax.rem(row + d, ndp), c) for d in range(ndp) for c in (me, other)][1:]
    for mate in mates:
        pl.semaphore_signal(
            barrier, inc=1, device_id={"ctx": upper * half + mate}, device_id_type=MESH
        )
    for d, c in twins:
        pl.semaphore_signal(barrier, inc=1, device_id={"dp": d, "ctx": c}, device_id_type=MESH)

    def chunk(ref, c, index, extra):
        return ref.at[c, index, pl.ds(0, share + (extra if c == chunks - 1 else 0))]

    def send(phase, c, source, target, extra=0):
        for mate in mates:
            pltpu.make_async_remote_copy(
                src_ref=chunk(source, c, mate, extra),
                dst_ref=chunk(target, c, place, extra),
                send_sem=send_sems.at[phase, c],
                recv_sem=recv_sems.at[phase, c],
                device_id={"ctx": upper * half + mate},
                device_id_type=MESH,
            ).start()
        target[c, place] = source[c, place]

    def landed(phase, c, target, extra=0):
        rest = chunk(target, c, pl.ds(0, half - 1), extra)
        pltpu.make_async_copy(rest, rest, recv_sems.at[phase, c]).wait()

    def left(phase, source, extra=0):
        for c in range(chunks):
            rest = chunk(source, c, pl.ds(0, half - 1), extra)
            pltpu.make_async_copy(rest, rest, send_sems.at[phase, c]).wait()

    def carry_copy(way, c):
        return pltpu.make_async_remote_copy(
            src_ref=sums.at[way, c],
            dst_ref=carry.at[way, c],
            send_sem=carry_send.at[way, c],
            recv_sem=carry_recv.at[way, c],
            device_id={"ctx": other},
            device_id_type=MESH,
        )

    def cross(way, c, arrived, giver):
        parts = [arrived[c, j, :share] for j in range(half)]
        sums[way, c] = functools.reduce(jnp.add, parts)

        @pl.when(giver)
        def _():
            carry_copy(way, c).start()
            carry[way, c] = jnp.zeros((share, LANES), F32)

    def crossed(way, c, giver):
        @pl.when(giver)
        def _():
            carry_copy(way, c).wait_send()

        @pl.when(jnp.logical_not(giver))
        def _():
            carry_copy(way, c).wait_recv()

    def scan(way, c, arrived, result, order):
        total = carry[way, c]
        for j in order:
            result[c, j, :share] = total
            total = total + arrived[c, j, :share]

    def lanes(p):
        return slice(p * LANES, (p + 1) * LANES)

    def place_of(p):
        return p // group, p % group * HEAD_DIM // share

    def pair_of(ref, p):
        c, first = place_of(p)
        return ref[c, first : first + slots, :share].reshape(HEAD_DIM, LANES)

    def put(ref, p, packed):
        c, first = place_of(p)
        ref[c, first : first + slots, :share] = packed.reshape(slots, share, LANES)

    loads[0].wait()
    loads[1].wait()
    for c in range(chunks):
        for p in range(c * group, (c + 1) * group):
            put(kv, p, pack(tn(k[:, lanes(p)], v[:, lanes(p)])))
        if c == 0:
            pl.semaphore_wait(barrier, len(mates) + len(twins))
        send(0, c, kv, kv_in)

    loads[2].wait()
    t = lax.broadcasted_iota(jnp.int32, (2 * GROUP, GROUP), 0) % GROUP
    causal = t >= lax.broadcasted_iota(jnp.int32, (2 * GROUP, GROUP), 1)

    def within(first, last):
        for p in range(pairs * first // 8, pairs * last // 8):
            s = nt(by_head(q[:, lanes(p)]), k[:, lanes(p)])
            s = jnp.where(causal, s, 0.0).astype(BF16)
            scores[p] = s
            q_turned[p] = q[:, lanes(p)].T
            attn[:, lanes(p)] = nn(side_by_side(s), by_head(v[:, lanes(p)]))

    ahead = range(half)
    lower = upper == 0
    within(0, 3)
    for c in range(chunks):
        landed(0, c, kv_in)
        cross(0, c, kv_in, lower)
        if c < chunks - 1:
            within(3 + c, 4 + c)
    for c in range(chunks):
        crossed(0, c, lower)
        scan(0, c, kv_in, prefix, ahead)
        send(1, c, prefix, state)
    within(2 + chunks, 8)
    loads[3].wait()
    loads[4].wait()

    squares = jnp.zeros((GROUP, LANES), F32)
    cross_sum = jnp.zeros((GROUP, LANES), F32)
    for c in range(chunks):
        landed(1, c, state)
        for p in range(c * group, (c + 1) * group):
            a = attn[:, lanes(p)] + nn(q[:, lanes(p)], unpack(pair_of(state, p)))
            attn[:, lanes(p)] = a
            squares += a * a
            cross_sum += a * (g[:, lanes(p)].astype(F32) * gain_ref[:, lanes(p)])
    inv = lax.rsqrt(jnp.sum(squares, 1, keepdims=True) / width + 1e-06)
    mean = jnp.sum(cross_sum, 1, keepdims=True) * inv / width
    tile = qd.shape[2] - share
    for c in range(chunks):
        for p in range(c * group, (c + 1) * group):
            normed = attn[:, lanes(p)] * inv
            gf = g[:, lanes(p)].astype(F32)
            ga = (inv * (gf * gain_ref[:, lanes(p)] - normed * mean)).astype(BF16)
            grad_attn[:, lanes(p)] = ga
            put(qd, p, pack(nn(q_turned[p], ga)))
            gain_tile = jnp.sum((gf * normed).reshape(GROUP // tile, tile, LANES), 0)
            for j in range(p * half // pairs, (p + 1) * half // pairs):
                qd[chunks - 1, j, share:] = gain_tile
        send(2, c, qd, qd_in, tile)

    def after(first, last):
        for p in range(pairs * first // 8, pairs * last // 8):
            normed = attn[:, lanes(p)] * inv
            o_out[:, lanes(p)] = (normed * gain_ref[:, lanes(p)]).astype(BF16)
            ga = grad_attn[:, lanes(p)]
            ga2 = by_head(ga)
            ds = jnp.where(causal, nt(ga2, v[:, lanes(p)]), 0.0).astype(BF16)
            gq = nn(side_by_side(ds), by_head(k[:, lanes(p)]))
            gq = gq + nt(ga, unpack(pair_of(state, p)))
            gq_out[:, lanes(p)] = gq.astype(BF16)
            gk_part[:, lanes(p)] = tn(ds, by_head(q[:, lanes(p)]))
            gv_part[:, lanes(p)] = tn(scores[p], ga2)

    back = range(half - 1, -1, -1)
    raised = upper == 1
    after(0, 2)
    for c in range(chunks):
        landed(2, c, qd_in, tile)
        cross(1, c, qd_in, raised)
        if c < chunks - 1:
            after(2 + c, 3 + c)
    slot = 2 * row + upper
    gains[slot] = functools.reduce(jnp.add, [qd_in[chunks - 1, j, share:] for j in range(half)])
    for d, c in twins:
        pltpu.make_async_remote_copy(
            src_ref=gains.at[slot],
            dst_ref=gains.at[slot],
            send_sem=gain_send,
            recv_sem=gain_recv,
            device_id={"dp": d, "ctx": c},
            device_id_type=MESH,
        ).start()
    rest = gains.at[pl.ds(0, len(twins))]
    for c in range(chunks):
        crossed(1, c, raised)
        scan(1, c, qd_in, suffix, back)
        if c == chunks - 1:
            pltpu.make_async_copy(rest, rest, gain_recv).wait()
            gain_sum = functools.reduce(jnp.add, [gains[j] for j in range(2 * ndp)])
            for j in range(half):
                suffix[c, j, share:] = gain_sum
        send(3, c, suffix, later, tile)
    after(1 + chunks, 8)

    pltpu.make_async_copy(rest, rest, gain_send).wait()
    left(0, kv)
    left(1, prefix)
    left(2, qd, tile)
    left(3, suffix, tile)
    for c in range(chunks):
        landed(3, c, later, tile)


def last_kernel(
    k, v, o, gq, gk_part, gv_part, later,
    out_hbm, gq_hbm, gk_hbm, gv_hbm, gg_hbm, gk_out, gv_out, gg, sems,
):
    stores = []

    def store(src, dst):
        stores.append(pltpu.make_async_copy(src, dst, sems.at[len(stores)]))
        stores[-1].start()

    store(o, out_hbm.at[0])
    store(gq, gq_hbm.at[0])
    width = k.shape[1]
    pairs = width // LANES
    chunks, half = later.shape[:2]
    group = pairs // chunks
    share = group * HEAD_DIM // half
    for p in range(pairs):
        gg[p : p + 1] = jnp.sum(later[chunks - 1, p * half // pairs, share:], 0, keepdims=True)
    store(gg, gg_hbm)
    for p in range(pairs):
        lanes = slice(p * LANES, (p + 1) * LANES)
        first = p % group * HEAD_DIM // share
        low = later[p // group, first : first + HEAD_DIM // share, :share]
        low = unpack(low.reshape(HEAD_DIM, LANES))
        gk_out[:, lanes] = (gk_part[:, lanes] + nt(v[:, lanes], low)).astype(BF16)
        gv_out[:, lanes] = (gv_part[:, lanes] + nn(k[:, lanes], low)).astype(BF16)
    store(gk_out, gk_hbm.at[0])
    store(gv_out, gv_hbm.at[0])
    for copy in stores:
        copy.wait()


def pinned(x):
    return pltpu.with_memory_space_constraint(x, pltpu.HBM)


def per_device(n, ndp, queries, keys, values, gain, grad_out):
    rows, width = queries.shape[1:]
    pairs = width // LANES
    half = n // 2
    chunks = 4 if pairs * HEAD_DIM // half >= 32 else 2
    share = pairs // chunks * HEAD_DIM // half
    gain_rows = width // LANES
    flat = jax.ShapeDtypeStruct((1, rows, width), BF16)
    low_out = jax.ShapeDtypeStruct((rows, width), BF16)
    full_out = jax.ShapeDtypeStruct((rows, width), F32)
    gain_out = jax.ShapeDtypeStruct((gain_rows, LANES), F32)
    hbm = pl.BlockSpec(memory_space=pltpu.HBM)
    vmem = pl.BlockSpec(memory_space=pltpu.VMEM)
    low = pltpu.VMEM((rows, width), BF16)
    full = pltpu.VMEM((rows, width), F32)
    part = pltpu.VMEM((chunks, half, share, LANES), F32)
    tile = 8
    wide = pltpu.VMEM((chunks, half, share + tile, LANES), F32)
    pair = pltpu.VMEM((2, chunks, share, LANES), F32)
    dma = pltpu.SemaphoreType.DMA
    k, v, o, gq, gk, gv, later = pl.pallas_call(
        functools.partial(scan_kernel, n, ndp),
        out_shape=[low_out] * 4
        + [full_out] * 2
        + [jax.ShapeDtypeStruct((chunks, half, share + tile, LANES), F32)],
        in_specs=[hbm] * 5,
        out_specs=[vmem] * 7,
        scratch_shapes=[low, low, pltpu.VMEM((1, width), F32), full, low]
        + [pltpu.VMEM((pairs, 2 * GROUP, GROUP), BF16), pltpu.VMEM((pairs, LANES, GROUP), BF16)]
        + [part] * 4
        + [wide] * 3
        + [pair, pair, pltpu.VMEM((2 * ndp, tile, LANES), F32)]
        + [dma((5,))] + [dma((4, chunks))] * 2 + [dma((2, chunks))] * 2 + [dma, dma],
        compiler_params=pltpu.CompilerParams(
            collective_id=0, has_side_effects=True, vmem_limit_bytes=32 * 2**20
        ),
        name="linear_attention",
    )(*(pinned(x) for x in (queries, keys, values, gain.reshape(1, width), grad_out)))
    out, gq, gk, gv, gg = pl.pallas_call(
        last_kernel,
        out_shape=[flat] * 4 + [gain_out],
        in_specs=[vmem] * 7,
        out_specs=[hbm] * 5,
        scratch_shapes=[low, low, pltpu.VMEM((gain_rows, LANES), F32), dma((5,))],
        compiler_params=pltpu.CompilerParams(vmem_limit_bytes=32 * 2**20),
        name="last_products",
    )(k, v, o, gq, gk, gv, later)
    return out, gq, gk, gv, gg.reshape(width)


def solution(mesh):
    spec = P("dp", "ctx", None)
    return jax.shard_map(
        functools.partial(per_device, mesh.shape["ctx"], mesh.shape["dp"]),
        mesh=mesh,
        in_specs=(spec, spec, spec, P(), spec),
        out_specs=(spec, spec, spec, spec, P()),
        check_vma=False,
    )
```

profile of v0, /device:TPU:0, one launch (start us, length us, event | category | flops | bytes accessed | tf_op | source)
XLA Modules:
  0.0 30.9 jit_solution(879897609392232886)
XLA Ops:
  0.6 29.1 %linear_attention.1 = (bf16[128,1024]{1,0:T(8,128)(2,1)S(1)}, bf16[128,1024]{1,0:T(8,128)(2,1)S(1)}, bf16[128,1024]{1,0:T(8,128)(2,1)S(1)}, bf16[128,1024]{1,0:T...) custom-call(bf16[1,128,1024]{2,1,0:T(8,128)(2,1)} %q_hbm.1, ...), custom_call_target="tpu_custom_call" | custom-call | tf_op jit(solution)/shard_map/linear_attention/pallas_call | solution.py:348
  29.7 1.2 %last_products.1 = (bf16[1,128,1024]{2,1,0:T(8,128)(2,1)}, bf16[1,128,1024]{2,1,0:T(8,128)(2,1)}, bf16[1,128,1024]{2,1,0:T(8,128)(2,1)}, bf16[1,128,1024]{2,1,0:T(8,128)(2,1)}, f32[8,128]{1,0:T(8,128)}) custom-call(bf16[128,1024]{1,0:T(8,128)(2,1)S(1)} %get-tuple-element.17.k, bf16[128,1024]{1,0:T(8,128)(2,1)S(1)} %get-tuple-element.18.v, ...), custom_call_target="tpu_custom_call" | custom-call | tf_op jit(solution)/shard_map/last_products/pallas_call | solution.py:366
where the time goes:
time: 31.1 us; the launch traced here: 30.9 us
  Pallas kernels  30.3 us (97%)
  between operations  0.64 us (2%)
    pallas_call x1, Pallas kernels, per_device(): pl.pallas_call(functools.partial(scan_kernel, n, ndp), out_shape=[low_out...  29.1 us
    pallas_call x1, Pallas kernels, per_device(): pl.pallas_call(last_kernel, out_shape=[flat] * 4 + [gain_out], in_specs=[...  1.2 us

commit v1 on v0

--- a/solution.py
+++ b/solution.py
@@ -88,10 +88,15 @@
 
     barrier = pltpu.get_barrier_semaphore()
     loads = []
-    arrays = (k_hbm.at[0], k), (v_hbm.at[0], v), (q_hbm.at[0], q), (g_hbm.at[0], g)
-    for i, (src, dst) in enumerate(arrays + ((gain_hbm, gain_ref),)):
-        loads.append(pltpu.make_async_copy(src, dst, in_sems.at[i]))
+
+    def load(src, dst):
+        loads.append(pltpu.make_async_copy(src, dst, in_sems.at[len(loads)]))
         loads[-1].start()
+
+    for c in range(chunks):
+        columns = slice(c * group * LANES, (c + 1) * group * LANES)
+        load(k_hbm.at[0, :, columns], k.at[:, columns])
+        load(v_hbm.at[0, :, columns], v.at[:, columns])
 
     mates = [flipped(place, mask, half) for mask in flips(half)]
     twins = [(lax.rem(row + d, ndp), c) for d in range(ndp) for c in (me, other)][1:]
@@ -174,16 +179,19 @@
         c, first = place_of(p)
         ref[c, first : first + slots, :share] = packed.reshape(slots, share, LANES)
 
-    loads[0].wait()
-    loads[1].wait()
-    for c in range(chunks):
+    for c in range(chunks):
+        loads[2 * c].wait()
+        loads[2 * c + 1].wait()
         for p in range(c * group, (c + 1) * group):
             put(kv, p, pack(tn(k[:, lanes(p)], v[:, lanes(p)])))
         if c == 0:
             pl.semaphore_wait(barrier, len(mates) + len(twins))
         send(0, c, kv, kv_in)
-
-    loads[2].wait()
+    load(q_hbm.at[0], q)
+    load(g_hbm.at[0], g)
+    load(gain_hbm, gain_ref)
+
+    loads[2 * chunks].wait()
     t = lax.broadcasted_iota(jnp.int32, (2 * GROUP, GROUP), 0) % GROUP
     causal = t >= lax.broadcasted_iota(jnp.int32, (2 * GROUP, GROUP), 1)
 
@@ -201,15 +209,13 @@
     for c in range(chunks):
         landed(0, c, kv_in)
         cross(0, c, kv_in, lower)
-        if c < chunks - 1:
-            within(3 + c, 4 + c)
     for c in range(chunks):
         crossed(0, c, lower)
         scan(0, c, kv_in, prefix, ahead)
         send(1, c, prefix, state)
-    within(2 + chunks, 8)
-    loads[3].wait()
-    loads[4].wait()
+    within(3, 8)
+    loads[2 * chunks + 1].wait()
+    loads[2 * chunks + 2].wait()
 
     squares = jnp.zeros((GROUP, LANES), F32)
     cross_sum = jnp.zeros((GROUP, LANES), F32)
@@ -254,8 +260,6 @@
     for c in range(chunks):
         landed(2, c, qd_in, tile)
         cross(1, c, qd_in, raised)
-        if c < chunks - 1:
-            after(2 + c, 3 + c)
     slot = 2 * row + upper
     gains[slot] = functools.reduce(jnp.add, [qd_in[chunks - 1, j, share:] for j in range(half)])
     for d, c in twins:
@@ -277,7 +281,7 @@
             for j in range(half):
                 suffix[c, j, share:] = gain_sum
         send(3, c, suffix, later, tile)
-    after(1 + chunks, 8)
+    after(2, 8)
 
     pltpu.make_async_copy(rest, rest, gain_send).wait()
     left(0, kv)
@@ -315,8 +319,10 @@
         low = unpack(low.reshape(HEAD_DIM, LANES))
         gk_out[:, lanes] = (gk_part[:, lanes] + nt(v[:, lanes], low)).astype(BF16)
         gv_out[:, lanes] = (gv_part[:, lanes] + nn(k[:, lanes], low)).astype(BF16)
-    store(gk_out, gk_hbm.at[0])
-    store(gv_out, gv_hbm.at[0])
+        if (p + 1) % (pairs // 2) == 0:
+            done = slice((p + 1 - pairs // 2) * LANES, (p + 1) * LANES)
+            store(gk_out.at[:, done], gk_hbm.at[0, :, done])
+            store(gv_out.at[:, done], gv_hbm.at[0, :, done])
     for copy in stores:
         copy.wait()
 
@@ -357,7 +363,7 @@
         + [part] * 4
         + [wide] * 3
         + [pair, pair, pltpu.VMEM((2 * ndp, tile, LANES), F32)]
-        + [dma((5,))] + [dma((4, chunks))] * 2 + [dma((2, chunks))] * 2 + [dma, dma],
+        + [dma((2 * chunks + 3,))] + [dma((4, chunks))] * 2 + [dma((2, chunks))] * 2 + [dma, dma],
         compiler_params=pltpu.CompilerParams(
             collective_id=0, has_side_effects=True, vmem_limit_bytes=32 * 2**20
         ),
@@ -368,7 +374,7 @@
         out_shape=[flat] * 4 + [gain_out],
         in_specs=[vmem] * 7,
         out_specs=[hbm] * 5,
-        scratch_shapes=[low, low, pltpu.VMEM((gain_rows, LANES), F32), dma((5,))],
+        scratch_shapes=[low, low, pltpu.VMEM((gain_rows, LANES), F32), dma((7,))],
         compiler_params=pltpu.CompilerParams(vmem_limit_bytes=32 * 2**20),
         name="last_products",
     )(k, v, o, gq, gk, gv, later)

time: 31.1 us -> 31.1 us (level)
  no operation moved by 1% of the time
where the time goes in v1:
time: 31.1 us; the launch traced here: 30.9 us
  Pallas kernels  30.3 us (97%)
  between operations  0.64 us (2%)
    pallas_call x1, Pallas kernels, per_device(): pl.pallas_call(functools.partial(scan_kernel, n, ndp), out_shape=[low_out...  29.2 us
    pallas_call x1, Pallas kernels, per_device(): pl.pallas_call(last_kernel, out_shape=[flat] * 4 + [gain_out], in_specs=[...  1.13 us

profile of v1, /device:TPU:0, one launch (start us, length us, event | category | flops | bytes accessed | tf_op | source)
XLA Modules:
  0.0 30.9 jit_solution(10501446696669444798)
XLA Ops:
  0.6 29.2 %linear_attention.1 = (bf16[128,1024]{1,0:T(8,128)(2,1)S(1)}, bf16[128,1024]{1,0:T(8,128)(2,1)S(1)}, bf16[128,1024]{1,0:T(8,128)(2,1)S(1)}, bf16[128,1024]{1,0:T...) custom-call(bf16[1,128,1024]{2,1,0:T(8,128)(2,1)} %q_hbm.1, ...), custom_call_target="tpu_custom_call" | custom-call | tf_op jit(solution)/shard_map/linear_attention/pallas_call | solution.py:354
  29.8 1.1 %last_products.1 = (bf16[1,128,1024]{2,1,0:T(8,128)(2,1)}, bf16[1,128,1024]{2,1,0:T(8,128)(2,1)}, bf16[1,128,1024]{2,1,0:T(8,128)(2,1)}, bf16[1,128,1024]{2,1,0:T(8,128)(2,1)}, f32[8,128]{1,0:T(8,128)}) custom-call(bf16[128,1024]{1,0:T(8,128)(2,1)S(1)} %get-tuple-element.17.k, bf16[128,1024]{1,0:T(8,128)(2,1)S(1)} %get-tuple-element.18.v, ...), custom_call_target="tpu_custom_call" | custom-call | tf_op jit(solution)/shard_map/last_products/pallas_call | solution.py:372

commit v2 on v1

--- a/solution.py
+++ b/solution.py
@@ -68,9 +68,9 @@
 
 def scan_kernel(
     n, ndp, q_hbm, k_hbm, v_hbm, gain_hbm, g_hbm,
-    k, v, o_out, gq_out, gk_part, gv_part, later,
-    q, g, gain_ref, attn, grad_attn, scores, q_turned,
-    kv, kv_in, prefix, state, qd, qd_in, suffix, sums, carry, gains,
+    o_out, gq_out, gk_out, gv_out, gg_out,
+    k, v, q, g, gain_ref, attn, grad_attn, scores, q_turned, gk_part, gv_part,
+    kv, kv_in, prefix, state, qd, qd_in, suffix, later, sums, carry, gains,
     in_sems, send_sems, recv_sems, carry_send, carry_recv, gain_send, gain_recv,
 ):
     me = lax.axis_index("ctx")
@@ -126,10 +126,21 @@
         rest = chunk(target, c, pl.ds(0, half - 1), extra)
         pltpu.make_async_copy(rest, rest, recv_sems.at[phase, c]).wait()
 
-    def left(phase, source, extra=0):
-        for c in range(chunks):
-            rest = chunk(source, c, pl.ds(0, half - 1), extra)
-            pltpu.make_async_copy(rest, rest, send_sems.at[phase, c]).wait()
+    pending = []
+
+    def left(phase, c, source, extra=0):
+        rest = chunk(source, c, pl.ds(0, half - 1), extra)
+        pltpu.make_async_copy(rest, rest, send_sems.at[phase, c]).wait()
+
+    def paced(phase, c, source, target, extra=0):
+        if c >= 2:
+            left(*pending.pop(0))
+        send(phase, c, source, target, extra)
+        pending.append((phase, c, source, extra))
+
+    def flush():
+        while pending:
+            left(*pending.pop(0))
 
     def carry_copy(way, c):
         return pltpu.make_async_remote_copy(
@@ -186,7 +197,7 @@
             put(kv, p, pack(tn(k[:, lanes(p)], v[:, lanes(p)])))
         if c == 0:
             pl.semaphore_wait(barrier, len(mates) + len(twins))
-        send(0, c, kv, kv_in)
+        paced(0, c, kv, kv_in)
     load(q_hbm.at[0], q)
     load(g_hbm.at[0], g)
     load(gain_hbm, gain_ref)
@@ -209,10 +220,11 @@
     for c in range(chunks):
         landed(0, c, kv_in)
         cross(0, c, kv_in, lower)
+    flush()
     for c in range(chunks):
         crossed(0, c, lower)
         scan(0, c, kv_in, prefix, ahead)
-        send(1, c, prefix, state)
+        paced(1, c, prefix, state)
     within(3, 8)
     loads[2 * chunks + 1].wait()
     loads[2 * chunks + 2].wait()
@@ -228,6 +240,7 @@
             cross_sum += a * (g[:, lanes(p)].astype(F32) * gain_ref[:, lanes(p)])
     inv = lax.rsqrt(jnp.sum(squares, 1, keepdims=True) / width + 1e-06)
     mean = jnp.sum(cross_sum, 1, keepdims=True) * inv / width
+    flush()
     tile = qd.shape[2] - share
     for c in range(chunks):
         for p in range(c * group, (c + 1) * group):
@@ -239,7 +252,10 @@
             gain_tile = jnp.sum((gf * normed).reshape(GROUP // tile, tile, LANES), 0)
             for j in range(p * half // pairs, (p + 1) * half // pairs):
                 qd[chunks - 1, j, share:] = gain_tile
-        send(2, c, qd, qd_in, tile)
+        if c < 2:
+            paced(2, c, qd, qd_in, tile)
+    for c in range(2, chunks):
+        paced(2, c, qd, qd_in, tile)
 
     def after(first, last):
         for p in range(pairs * first // 8, pairs * last // 8):
@@ -271,6 +287,7 @@
             device_id={"dp": d, "ctx": c},
             device_id_type=MESH,
         ).start()
+    flush()
     rest = gains.at[pl.ds(0, len(twins))]
     for c in range(chunks):
         crossed(1, c, raised)
@@ -280,49 +297,30 @@
             gain_sum = functools.reduce(jnp.add, [gains[j] for j in range(2 * ndp)])
             for j in range(half):
                 suffix[c, j, share:] = gain_sum
-        send(3, c, suffix, later, tile)
+        paced(3, c, suffix, later, tile)
     after(2, 8)
 
     pltpu.make_async_copy(rest, rest, gain_send).wait()
-    left(0, kv)
-    left(1, prefix)
-    left(2, qd, tile)
-    left(3, suffix, tile)
+    flush()
     for c in range(chunks):
         landed(3, c, later, tile)
-
-
-def last_kernel(
-    k, v, o, gq, gk_part, gv_part, later,
-    out_hbm, gq_hbm, gk_hbm, gv_hbm, gg_hbm, gk_out, gv_out, gg, sems,
-):
+        for p in range(c * group, (c + 1) * group):
+            low = unpack(pair_of(later, p))
+            gk = gk_part[:, lanes(p)] + nt(v[:, lanes(p)], low)
+            gv = gv_part[:, lanes(p)] + nn(k[:, lanes(p)], low)
+            gk_out[:, lanes(p)] = gk.astype(BF16)
+            gv_out[:, lanes(p)] = gv.astype(BF16)
+    for p in range(pairs):
+        gain_rows = later[chunks - 1, p * half // pairs, share:]
+        gg_out[p : p + 1] = jnp.sum(gain_rows, 0, keepdims=True)
+
+
+def last_kernel(o, gq, gk, gv, gg, out_hbm, gq_hbm, gk_hbm, gv_hbm, gg_hbm, sems):
     stores = []
-
-    def store(src, dst):
-        stores.append(pltpu.make_async_copy(src, dst, sems.at[len(stores)]))
+    arrays = (o, out_hbm.at[0]), (gq, gq_hbm.at[0]), (gk, gk_hbm.at[0]), (gv, gv_hbm.at[0])
+    for i, (src, dst) in enumerate(arrays + ((gg, gg_hbm),)):
+        stores.append(pltpu.make_async_copy(src, dst, sems.at[i]))
         stores[-1].start()
-
-    store(o, out_hbm.at[0])
-    store(gq, gq_hbm.at[0])
-    width = k.shape[1]
-    pairs = width // LANES
-    chunks, half = later.shape[:2]
-    group = pairs // chunks
-    share = group * HEAD_DIM // half
-    for p in range(pairs):
-        gg[p : p + 1] = jnp.sum(later[chunks - 1, p * half // pairs, share:], 0, keepdims=True)
-    store(gg, gg_hbm)
-    for p in range(pairs):
-        lanes = slice(p * LANES, (p + 1) * LANES)
-        first = p % group * HEAD_DIM // share
-        low = later[p // group, first : first + HEAD_DIM // share, :share]
-        low = unpack(low.reshape(HEAD_DIM, LANES))
-        gk_out[:, lanes] = (gk_part[:, lanes] + nt(v[:, lanes], low)).astype(BF16)
-        gv_out[:, lanes] = (gv_part[:, lanes] + nn(k[:, lanes], low)).astype(BF16)
-        if (p + 1) % (pairs // 2) == 0:
-            done = slice((p + 1 - pairs // 2) * LANES, (p + 1) * LANES)
-            store(gk_out.at[:, done], gk_hbm.at[0, :, done])
-            store(gv_out.at[:, done], gv_hbm.at[0, :, done])
     for copy in stores:
         copy.wait()
 
@@ -340,7 +338,6 @@
     gain_rows = width // LANES
     flat = jax.ShapeDtypeStruct((1, rows, width), BF16)
     low_out = jax.ShapeDtypeStruct((rows, width), BF16)
-    full_out = jax.ShapeDtypeStruct((rows, width), F32)
     gain_out = jax.ShapeDtypeStruct((gain_rows, LANES), F32)
     hbm = pl.BlockSpec(memory_space=pltpu.HBM)
     vmem = pl.BlockSpec(memory_space=pltpu.VMEM)
@@ -351,19 +348,21 @@
     wide = pltpu.VMEM((chunks, half, share + tile, LANES), F32)
     pair = pltpu.VMEM((2, chunks, share, LANES), F32)
     dma = pltpu.SemaphoreType.DMA
-    k, v, o, gq, gk, gv, later = pl.pallas_call(
+    results = pl.pallas_call(
         functools.partial(scan_kernel, n, ndp),
-        out_shape=[low_out] * 4
-        + [full_out] * 2
-        + [jax.ShapeDtypeStruct((chunks, half, share + tile, LANES), F32)],
+        out_shape=[low_out] * 4 + [gain_out],
         in_specs=[hbm] * 5,
-        out_specs=[vmem] * 7,
-        scratch_shapes=[low, low, pltpu.VMEM((1, width), F32), full, low]
-        + [pltpu.VMEM((pairs, 2 * GROUP, GROUP), BF16), pltpu.VMEM((pairs, LANES, GROUP), BF16)]
+        out_specs=[vmem] * 5,
+        scratch_shapes=[low] * 4
+        + [pltpu.VMEM((1, width), F32), full, low, pltpu.VMEM((pairs, 2 * GROUP, GROUP), BF16)]
+        + [pltpu.VMEM((pairs, LANES, GROUP), BF16), full, full]
         + [part] * 4
-        + [wide] * 3
+        + [wide] * 4
         + [pair, pair, pltpu.VMEM((2 * ndp, tile, LANES), F32)]
-        + [dma((2 * chunks + 3,))] + [dma((4, chunks))] * 2 + [dma((2, chunks))] * 2 + [dma, dma],
+        + [dma((2 * chunks + 3,))]
+        + [dma((4, chunks))] * 2
+        + [dma((2, chunks))] * 2
+        + [dma, dma],
         compiler_params=pltpu.CompilerParams(
             collective_id=0, has_side_effects=True, vmem_limit_bytes=32 * 2**20
         ),
@@ -372,12 +371,12 @@
     out, gq, gk, gv, gg = pl.pallas_call(
         last_kernel,
         out_shape=[flat] * 4 + [gain_out],
-        in_specs=[vmem] * 7,
+        in_specs=[vmem] * 5,
         out_specs=[hbm] * 5,
-        scratch_shapes=[low, low, pltpu.VMEM((gain_rows, LANES), F32), dma((7,))],
+        scratch_shapes=[dma((5,))],
         compiler_params=pltpu.CompilerParams(vmem_limit_bytes=32 * 2**20),
-        name="last_products",
-    )(k, v, o, gq, gk, gv, later)
+        name="store_results",
+    )(*results)
     return out, gq, gk, gv, gg.reshape(width)
 
 

time: 31.1 us -> 33 us (1.061)
  Pallas kernels: 30.3 us -> 32.2 us
    pallas_call x1, Pallas kernels: 29.2 us -> 31.2 us  [per_device(): pl.pallas_call(functools.partial(scan_kernel, n, ndp), out_shape=[low_out...]
where the time goes in v2:
time: 33 us; the launch traced here: 32.9 us
  Pallas kernels  32.2 us (98%)
  between operations  0.64 us (2%)
    pallas_call x1, Pallas kernels, per_device(): pl.pallas_call(functools.partial(scan_kernel, n, ndp), out_shape=[low_out...  31.2 us
    pallas_call x1, Pallas kernels, per_device(): pl.pallas_call(last_kernel, out_shape=[flat] * 4 + [gain_out], in_specs=[...  1.01 us

profile of v2, /device:TPU:0, one launch (start us, length us, event | category | flops | bytes accessed | tf_op | source)
XLA Modules:
  0.0 32.9 jit_solution(4210255572788065376)
XLA Ops:
  0.6 31.2 %linear_attention.1 = (bf16[128,1024]{1,0:T(8,128)(2,1)S(1)}, bf16[128,1024]{1,0:T(8,128)(2,1)S(1)}, bf16[128,1024]{1,0:T(8,128)(2,1)S(1)}, bf16[128,1024]{1,0:T(8,128)(2,1)S(1)}, f32[8,128]{1,0:T(8,128)S(1)}) custom-call(bf16[1,128,1024]{2,1,0:T(8,128)(2,1)} %q_hbm.1, bf16[1,128,1024]{2,1,0:T(8,128)(2,1)} %k_hbm.1, bf16[1,128,1024]{2,1,0:T(8,128)(2,1)} %v_hbm.1, ...), custom_call_target="tpu_custom_call" | custom-call | tf_op jit(solution)/shard_map/linear_attention/pallas_call | solution.py:351
  31.9 1.0 %store_results.1 = (bf16[1,128,1024]{2,1,0:T(8,128)(2,1)}, bf16[1,128,1024]{2,1,0:T(8,128)(2,1)}, bf16[1,128,1024]{2,1,0:T(8,128)(2,1)}, bf16[1,128,1024]{2,1,0:T(8,128)(2,1)}, f32[8,128]{1,0:T(8,128)}) custom-call(bf16[128,1024]{1,0:T(8,128)(2,1)S(1)} %get-tuple-element.15.o, bf16[128,1024]{1,0:T(8,128)(2,1)S(1)} %get-tuple-element.16.gq, ...), custom_call_target="tpu_custom_call" | custom-call | tf_op jit(solution)/shard_map/store_results/pallas_call | solution.py:371

commit v3 on v1

--- a/solution.py
+++ b/solution.py
@@ -87,17 +87,6 @@
     other = lax.rem(me + half, n)
 
     barrier = pltpu.get_barrier_semaphore()
-    loads = []
-
-    def load(src, dst):
-        loads.append(pltpu.make_async_copy(src, dst, in_sems.at[len(loads)]))
-        loads[-1].start()
-
-    for c in range(chunks):
-        columns = slice(c * group * LANES, (c + 1) * group * LANES)
-        load(k_hbm.at[0, :, columns], k.at[:, columns])
-        load(v_hbm.at[0, :, columns], v.at[:, columns])
-
     mates = [flipped(place, mask, half) for mask in flips(half)]
     twins = [(lax.rem(row + d, ndp), c) for d in range(ndp) for c in (me, other)][1:]
     for mate in mates:
@@ -106,6 +95,17 @@
         )
     for d, c in twins:
         pl.semaphore_signal(barrier, inc=1, device_id={"dp": d, "ctx": c}, device_id_type=MESH)
+
+    loads = []
+
+    def load(src, dst):
+        loads.append(pltpu.make_async_copy(src, dst, in_sems.at[len(loads)]))
+        loads[-1].start()
+
+    for c in range(chunks):
+        columns = slice(c * group * LANES, (c + 1) * group * LANES)
+        load(k_hbm.at[0, :, columns], k.at[:, columns])
+        load(v_hbm.at[0, :, columns], v.at[:, columns])
 
     def chunk(ref, c, index, extra):
         return ref.at[c, index, pl.ds(0, share + (extra if c == chunks - 1 else 0))]
@@ -335,7 +335,7 @@
     rows, width = queries.shape[1:]
     pairs = width // LANES
     half = n // 2
-    chunks = 4 if pairs * HEAD_DIM // half >= 32 else 2
+    chunks = 2
     share = pairs // chunks * HEAD_DIM // half
     gain_rows = width // LANES
     flat = jax.ShapeDtypeStruct((1, rows, width), BF16)

time: 31.1 us -> 31.4 us (level)
    pallas_call x1, Pallas kernels: 29.2 us -> 29.5 us  [per_device(): pl.pallas_call(functools.partial(scan_kernel, n, ndp), out_shape=[low_out...]
where the time goes in v3:
time: 31.4 us; the launch traced here: 31.3 us
  Pallas kernels  30.6 us (97%)
  between operations  0.64 us (2%)
    pallas_call x1, Pallas kernels, per_device(): pl.pallas_call(functools.partial(scan_kernel, n, ndp), out_shape=[low_out...  29.5 us
    pallas_call x1, Pallas kernels, per_device(): pl.pallas_call(last_kernel, out_shape=[flat] * 4 + [gain_out], in_specs=[...  1.13 us

profile of v3, /device:TPU:0, one launch (start us, length us, event | category | flops | bytes accessed | tf_op | source)
XLA Modules:
  0.0 31.3 jit_solution(9605120547991702816)
XLA Ops:
  0.6 29.5 %linear_attention.1 = (bf16[128,1024]{1,0:T(8,128)(2,1)S(1)}, bf16[128,1024]{1,0:T(8,128)(2,1)S(1)}, bf16[128,1024]{1,0:T(8,128)(2,1)S(1)}, bf16[128,1024]{1,0:T...) custom-call(bf16[1,128,1024]{2,1,0:T(8,128)(2,1)} %q_hbm.1, ...), custom_call_target="tpu_custom_call" | custom-call | tf_op jit(solution)/shard_map/linear_attention/pallas_call | solution.py:354
  30.1 1.1 %last_products.1 = (bf16[1,128,1024]{2,1,0:T(8,128)(2,1)}, bf16[1,128,1024]{2,1,0:T(8,128)(2,1)}, bf16[1,128,1024]{2,1,0:T(8,128)(2,1)}, bf16[1,128,1024]{2,1,0:T(8,128)(2,1)}, f32[8,128]{1,0:T(8,128)}) custom-call(bf16[128,1024]{1,0:T(8,128)(2,1)S(1)} %get-tuple-element.17.k, bf16[128,1024]{1,0:T(8,128)(2,1)S(1)} %get-tuple-element.18.v, ...), custom_call_target="tpu_custom_call" | custom-call | tf_op jit(solution)/shard_map/last_products/pallas_call | solution.py:372

commit v4 on v3

--- a/solution.py
+++ b/solution.py
@@ -69,7 +69,7 @@
 def scan_kernel(
     n, ndp, q_hbm, k_hbm, v_hbm, gain_hbm, g_hbm,
     k, v, o_out, gq_out, gk_part, gv_part, later,
-    q, g, gain_ref, attn, grad_attn, scores, q_turned,
+    q, g, gain_ref, attn, grad_attn, scores, q_turned, grad_norm,
     kv, kv_in, prefix, state, qd, qd_in, suffix, sums, carry, gains,
     in_sems, send_sems, recv_sems, carry_send, carry_recv, gain_send, gain_recv,
 ):
@@ -217,6 +217,9 @@
     loads[2 * chunks + 1].wait()
     loads[2 * chunks + 2].wait()
 
+    for p in range(pairs):
+        grad_norm[:, lanes(p)] = g[:, lanes(p)].astype(F32) * gain_ref[:, lanes(p)]
+
     squares = jnp.zeros((GROUP, LANES), F32)
     cross_sum = jnp.zeros((GROUP, LANES), F32)
     for c in range(chunks):
@@ -225,17 +228,17 @@
             a = attn[:, lanes(p)] + nn(q[:, lanes(p)], unpack(pair_of(state, p)))
             attn[:, lanes(p)] = a
             squares += a * a
-            cross_sum += a * (g[:, lanes(p)].astype(F32) * gain_ref[:, lanes(p)])
+            cross_sum += a * grad_norm[:, lanes(p)]
     inv = lax.rsqrt(jnp.sum(squares, 1, keepdims=True) / width + 1e-06)
     mean = jnp.sum(cross_sum, 1, keepdims=True) * inv / width
     tile = qd.shape[2] - share
     for c in range(chunks):
         for p in range(c * group, (c + 1) * group):
             normed = attn[:, lanes(p)] * inv
-            gf = g[:, lanes(p)].astype(F32)
-            ga = (inv * (gf * gain_ref[:, lanes(p)] - normed * mean)).astype(BF16)
+            ga = (inv * (grad_norm[:, lanes(p)] - normed * mean)).astype(BF16)
             grad_attn[:, lanes(p)] = ga
             put(qd, p, pack(nn(q_turned[p], ga)))
+            gf = g[:, lanes(p)].astype(F32)
             gain_tile = jnp.sum((gf * normed).reshape(GROUP // tile, tile, LANES), 0)
             for j in range(p * half // pairs, (p + 1) * half // pairs):
                 qd[chunks - 1, j, share:] = gain_tile
@@ -335,7 +338,7 @@
     rows, width = queries.shape[1:]
     pairs = width // LANES
     half = n // 2
-    chunks = 2
+    chunks = 4 if pairs * HEAD_DIM // half >= 32 else 2
     share = pairs // chunks * HEAD_DIM // half
     gain_rows = width // LANES
     flat = jax.ShapeDtypeStruct((1, rows, width), BF16)
@@ -360,6 +363,7 @@
         out_specs=[vmem] * 7,
         scratch_shapes=[low, low, pltpu.VMEM((1, width), F32), full, low]
         + [pltpu.VMEM((pairs, 2 * GROUP, GROUP), BF16), pltpu.VMEM((pairs, LANES, GROUP), BF16)]
+        + [full]
         + [part] * 4
         + [wide] * 3
         + [pair, pair, pltpu.VMEM((2 * ndp, tile, LANES), F32)]

time: 31.4 us -> 31.1 us (level)
    pallas_call x1, Pallas kernels: 29.5 us -> 29.1 us  [per_device(): pl.pallas_call(functools.partial(scan_kernel, n, ndp), out_shape=[low_out...]
where the time goes in v4:
time: 31.1 us; the launch traced here: 30.9 us
  Pallas kernels  30.3 us (97%)
  between operations  0.64 us (2%)
    pallas_call x1, Pallas kernels, per_device(): pl.pallas_call(functools.partial(scan_kernel, n, ndp), out_shape=[low_out...  29.1 us
    pallas_call x1, Pallas kernels, per_device(): pl.pallas_call(last_kernel, out_shape=[flat] * 4 + [gain_out], in_specs=[...  1.13 us

profile of v4, /device:TPU:0, one launch (start us, length us, event | category | flops | bytes accessed | tf_op | source)
XLA Modules:
  0.0 30.9 jit_solution(1395279262065022716)
XLA Ops:
  0.6 29.1 %linear_attention.1 = (bf16[128,1024]{1,0:T(8,128)(2,1)S(1)}, bf16[128,1024]{1,0:T(8,128)(2,1)S(1)}, bf16[128,1024]{1,0:T(8,128)(2,1)S(1)}, bf16[128,1024]{1,0:T...) custom-call(bf16[1,128,1024]{2,1,0:T(8,128)(2,1)} %q_hbm.1, ...), custom_call_target="tpu_custom_call" | custom-call | tf_op jit(solution)/shard_map/linear_attention/pallas_call | solution.py:357
  29.8 1.1 %last_products.1 = (bf16[1,128,1024]{2,1,0:T(8,128)(2,1)}, bf16[1,128,1024]{2,1,0:T(8,128)(2,1)}, bf16[1,128,1024]{2,1,0:T(8,128)(2,1)}, bf16[1,128,1024]{2,1,0:T(8,128)(2,1)}, f32[8,128]{1,0:T(8,128)}) custom-call(bf16[128,1024]{1,0:T(8,128)(2,1)S(1)} %get-tuple-element.17.k, bf16[128,1024]{1,0:T(8,128)(2,1)S(1)} %get-tuple-element.18.v, ...), custom_call_target="tpu_custom_call" | custom-call | tf_op jit(solution)/shard_map/last_products/pallas_call | solution.py:376
